TPU v7x, 512 devices: a whole 4x8x8 slice. The times are simulated.
512 devices in a mesh: prompt: 32 (over z, x), sample: 16 (over y, core).
Axes of the slice: x: 4, y: 8, z: 8, core: 2. Of those that a mesh axis runs over, the one named last changes fastest.
Arguments:
- prompt_q: bfloat16 [8192, 2048], P(('prompt', 'sample')), parts along dimension 0, may hold values from -6 to 6
- prompt_k: bfloat16 [8192, 512], P(('prompt', 'sample')), parts along dimension 0, may hold values from -6 to 6
- prompt_value_rows: bfloat16 [8192, 512], P(('prompt', 'sample')), parts along dimension 0, may hold values from -5 to 5
- prompt_dout: bfloat16 [8192, 2048], P(('prompt', 'sample')), parts along dimension 0, may hold values from -5 to 5
- comp_q: bfloat16 [512, 128, 2048], P(('prompt', 'sample')), parts along dimension 0, may hold values from -6 to 6
- completion_keys: bfloat16 [512, 128, 512], P(('prompt', 'sample')), parts along dimension 0, may hold values from -5 to 5
- completion_values: bfloat16 [512, 128, 512], P(('prompt', 'sample')), parts along dimension 0, may hold values from -5 to 5
- comp_dout: bfloat16 [512, 128, 2048], P(('prompt', 'sample')), parts along dimension 0, may hold values from -5 to 5
- comp_lengths: int32 [512], P(('prompt', 'sample')), parts along dimension 0, may hold values from 32 to 128, as said below
- prompt_length: int32 [32], P('prompt'), parts along dimension 0, may hold values from 224 to 256, as said below
Outputs:
- prompt_dq: bfloat16 [8192, 2048], P(('prompt', 'sample')), parts along dimension 0
- prompt_dk: bfloat16 [8192, 512], P(('prompt', 'sample')), parts along dimension 0
- prompt_dv: bfloat16 [8192, 512], P(('prompt', 'sample')), parts along dimension 0
- comp_dq: bfloat16 [512, 128, 2048], P(('prompt', 'sample')), parts along dimension 0
- comp_dk: bfloat16 [512, 128, 512], P(('prompt', 'sample')), parts along dimension 0
- comp_dv: bfloat16 [512, 128, 512], P(('prompt', 'sample')), parts along dimension 0
There are 32 independent parts, one for each index of `prompt`. A program takes and returns all parts, laid end to end along the dimension named above; each array names one. Nothing has to cross between parts.
Inputs may be any that keep to these rules, and one draw needn't show every extreme that they name: `comp_lengths`: one completion of every prompt has exactly 128 tokens. Prompt rows at and after prompt_length are padding.
All inputs are finite; a program needn't handle non-finite values.
Results may differ from a plain program's by a relative error of at most 0.012.
The roundings to bfloat16 on the way count: a program that leaves them out, or rounds other values in their place, can miss the bound.
Values may be sent and summed in bfloat16 or wider, within the bound.
No kernel may reach another device: no remote copies, remote signals or barrier semaphores. Data moves between devices by JAX's collectives and lax.ppermute only.
A program may use at most 64 MiB of HBM per device.

v0:
```python
import jax
import jax.numpy as jnp
from jax import lax
from jax.experimental import pallas as pl
from jax.experimental.pallas import tpu as pltpu
from jax.sharding import PartitionSpec as P

QUERY_HEADS = 16
KEY_VALUE_HEADS = 4
HEAD_DIM = 128
GROUP = QUERY_HEADS // KEY_VALUE_HEADS
SCALE = HEAD_DIM ** (-0.5)
LOG2E = 1.4426950408889634
CHIPS = 8
CORES = 2
DEVICES = CHIPS * CORES
MASKED = -1e30

HALF_HEADS = KEY_VALUE_HEADS // CORES
HALF_WIDTH = HALF_HEADS * HEAD_DIM
HALF_COLUMNS = HALF_WIDTH * GROUP

SLOTS = 16
ROWS = 128
KEYS = DEVICES * SLOTS

PROMPT_ROW = ROWS
EXTRA_ROW = ROWS + SLOTS
QUERY_BLOCK = EXTRA_ROW + SLOTS
OTHER_BLOCK = EXTRA_ROW + ROWS // 2

ORDER = [
    chip % CHIPS * CORES + core
    for step in range(CHIPS)
    for core in range(CORES)
    for chip in [3 * step + core * (CHIPS // CORES)]
]
PLACE = [ORDER.index(device) for device in range(DEVICES)]

NT = ((1,), (1,))
NN = ((1,), (0,))
VMEM = pl.BlockSpec(memory_space=pltpu.VMEM)
SMEM = pl.BlockSpec(memory_space=pltpu.SMEM)
ANY = pl.BlockSpec(memory_space=pl.ANY)


def dot(a, b, contract):
    return lax.dot_general(a, b, (contract, ((), ())), preferred_element_type=jnp.float32)


def own_core():
    return lax.rem(lax.axis_index("sample"), CORES)


def columns_of(core, width):
    return pl.ds(pl.multiple_of(core * width, HEAD_DIM), width)


def run(copies):
    for copy in copies:
        copy.start()
    for copy in copies:
        copy.wait()


def stage_kernel(k_ref, v_ref, out_ref, kv_ref, sems):
    run(
        [
            pltpu.make_async_copy(source, kv_ref.at[n], sems.at[n])
            for n, source in enumerate((k_ref, v_ref))
        ]
    )
    for core in range(CORES):
        columns = slice(core * HALF_WIDTH, (core + 1) * HALF_WIDTH)
        rows = jnp.concatenate([kv_ref[0, :, columns], kv_ref[1, :, columns]], axis=1)
        for chip in range(CHIPS):
            out_ref[PLACE[chip * CORES + core]] = rows


def packed(ref, n):
    return ref.at[EXTRA_ROW:OTHER_BLOCK, n * HALF_WIDTH : (n + 1) * HALF_WIDTH]


def split_kernel(clen_ref, q_ref, do_ref, pq_ref, pdo_ref, ck_ref, cv_ref, _, *refs):
    core = own_core()
    sems = refs[-1]
    copies = []
    for n, half in enumerate((core, 1 - core)):
        query_block, other_block = refs[2 * n : 2 * n + 2]
        wide, narrow = columns_of(half, HALF_COLUMNS), columns_of(half, HALF_WIDTH)
        pairs = [
            (q_ref.at[:, wide], query_block.at[:ROWS]),
            (pq_ref.at[:, wide], query_block.at[PROMPT_ROW:EXTRA_ROW]),
            (do_ref.at[:, wide], other_block.at[:ROWS]),
            (pdo_ref.at[:, wide], other_block.at[PROMPT_ROW:EXTRA_ROW]),
        ]
        for k, source in enumerate((ck_ref, cv_ref)):
            for part in range(2):
                rows = slice(part * ROWS // 2, (part + 1) * ROWS // 2)
                pairs.append((source.at[rows, narrow], packed(other_block, 2 * k + part)))
        copies += [
            pltpu.make_async_copy(source, place, sems.at[n * len(pairs) + k])
            for k, (source, place) in enumerate(pairs)
        ]
    for copy in copies:
        copy.start()
    length = jnp.full((SLOTS, HALF_COLUMNS), clen_ref[0], jnp.int32).astype(jnp.float32)
    for query_block in refs[0:4:2]:
        query_block[EXTRA_ROW:QUERY_BLOCK] = length.astype(jnp.bfloat16)
    for copy in copies:
        copy.wait()


def head_columns(ref, first_row, count, head):
    parts = [
        ref[
            first_row : first_row + count,
            (head * GROUP + g) * HEAD_DIM : (head * GROUP + g + 1) * HEAD_DIM,
        ]
        for g in range(GROUP)
    ]
    return jnp.concatenate(parts, axis=0)


def own_rows(ref, head, first):
    parts = [
        packed(ref, first + part)[:, head * HEAD_DIM : (head + 1) * HEAD_DIM]
        for part in range(2)
    ]
    return jnp.concatenate(parts, axis=0)


FACTOR = SCALE * LOG2E


def exponentials(scores, peak):
    return jnp.exp2(scores * FACTOR - peak * FACTOR)


def top(scores):
    return jnp.max(scores, axis=0, keepdims=True)


def column_sum(values):
    return jnp.sum(values, axis=0, keepdims=True)


def own_allowed():
    key = lax.broadcasted_iota(jnp.int32, (ROWS, ROWS), 0)
    return key <= lax.broadcasted_iota(jnp.int32, (ROWS, ROWS), 1)


def own_kernel(query_block, other_block, share_ref):
    allowed = own_allowed()
    for head in range(HALF_HEADS):
        q = head_columns(query_block, 0, ROWS, head)
        do = head_columns(other_block, 0, ROWS, head)
        scores = dot(own_rows(other_block, head, 0), q, NT)
        soft_grad = dot(own_rows(other_block, head, 2), do, NT)
        for start in range(0, GROUP * ROWS, ROWS):
            lanes = slice(start, start + ROWS)
            piece = jnp.where(allowed, scores[:, lanes], MASKED)
            peak = top(piece)
            terms = exponentials(piece, peak)
            share_ref[head, 0:1, lanes] = peak
            share_ref[head, 1:2, lanes] = column_sum(terms)
            share_ref[head, 2:3, lanes] = column_sum(terms * soft_grad[:, lanes])


class Attention:
    def __init__(self, plen_ref, mine_q, mine_other, got_q, got_other, kv_ref, *shares):
        self.shares = shares
        self.sides = (mine_q, mine_other), (got_q, got_other)
        self.kv_ref = kv_ref
        plen = plen_ref[0]
        own = lax.axis_index("sample")
        other = own + 1 - 2 * own_core()
        row_lane = lax.broadcasted_iota(jnp.int32, (1, ROWS), 1)
        self.valid = []
        for ref, _ in self.sides:
            length = ref[EXTRA_ROW:QUERY_BLOCK, :ROWS].astype(jnp.float32)[0:1]
            live = row_lane.astype(jnp.float32) < length
            self.valid.append(jnp.where(live, 1.0, 0.0).astype(jnp.float32))
        self.safe = KEYS - 2 * SLOTS
        self.tail_ok = (
            lax.broadcasted_iota(jnp.int32, (2 * SLOTS, ROWS), 0) + self.safe < plen
        )
        self.own_ok = own_allowed()
        lanes = CORES * GROUP * SLOTS
        lane = lax.broadcasted_iota(jnp.int32, (1, lanes), 1)
        device = jnp.where(lane < GROUP * SLOTS, own, other)
        global_row = device * SLOTS + lax.rem(lane, SLOTS)
        self.prompt_valid = jnp.where(global_row < plen, 1.0, 0.0).astype(jnp.float32)
        self.prompt_ok = lax.broadcasted_iota(jnp.int32, (KEYS, lanes), 0) <= global_row

    def prompt_rows(self, start):
        parts = [
            self.kv_ref[PLACE[device], :, start : start + HEAD_DIM] for device in range(DEVICES)
        ]
        return jnp.concatenate(parts, axis=0)

    def products(self, head, side):
        keys = self.prompt_rows(head * HEAD_DIM)
        values = self.prompt_rows(HALF_WIDTH + head * HEAD_DIM)
        if side < CORES:
            query_block, other_block = self.sides[side]
            if not self.shares:
                keys = jnp.concatenate([keys, own_rows(other_block, head, 0)], axis=0)
                values = jnp.concatenate([values, own_rows(other_block, head, 2)], axis=0)
            q = head_columns(query_block, 0, ROWS, head)
            do = head_columns(other_block, 0, ROWS, head)
        else:
            q, do = (
                jnp.concatenate(
                    [head_columns(ref, PROMPT_ROW, SLOTS, head) for ref in blocks], axis=0
                )
                for blocks in zip(*self.sides)
            )
        return dot(keys, q, NT), dot(values, do, NT), (keys, q, do)

    def weights(self, head, side, scores, soft_grad):
        pieces = []
        for start in range(0, scores.shape[1], ROWS):
            lanes = slice(start, start + ROWS)
            piece, piece_grad = scores[:, lanes], soft_grad[:, lanes]
            if side < CORES:
                parts = [piece[: self.safe], jnp.where(self.tail_ok, piece[self.safe : KEYS], MASKED)]
                if not self.shares:
                    parts.append(jnp.where(self.own_ok, piece[KEYS:], MASKED))
                piece = jnp.concatenate(parts, axis=0)
                valid = self.valid[side]
            else:
                piece = jnp.where(self.prompt_ok, piece, MASKED)
                valid = self.prompt_valid
            peak = top(piece)
            own_total = own_delta = 0.0
            if side < CORES and self.shares:
                own_peak, own_total, own_delta = (
                    self.shares[side][head, n : n + 1, lanes] for n in range(3)
                )
                peak = jnp.maximum(peak, own_peak)
                weight = exponentials(own_peak, peak)
                own_total, own_delta = own_total * weight, own_delta * weight
            terms = exponentials(piece, peak)
            scale = valid / (column_sum(terms) + own_total)
            soft = terms * scale
            soft_b = soft.astype(jnp.bfloat16)
            delta = column_sum(soft_b.astype(jnp.float32) * piece_grad) + own_delta * scale
            pieces.append((soft_b, (soft * (piece_grad - delta)).astype(jnp.bfloat16)))
        return [jnp.concatenate(part, axis=1) for part in zip(*pieces)]

    def units(self):
        todo = [(head, side) for head in range(HALF_HEADS) for side in (0, 1, 2)]
        following = self.products(*todo[0])
        for n, (head, side) in enumerate(todo):
            scores, soft_grad, operands = following
            if n + 1 < len(todo):
                following = self.products(*todo[n + 1])
            yield head, side, operands, *self.weights(head, side, scores, soft_grad)


def attend_kernel(*refs):
    part_ref = refs[-1]
    dk = dv = None
    for head, side, (_, q, do), soft_b, grad_b in Attention(*refs[:8]).units():
        more_dv = dot(soft_b, do, NN)
        more_dk = dot(grad_b, q, NN)
        dv = more_dv if side == 0 else dv + more_dv
        dk = more_dk if side == 0 else dk + more_dk
        if side == CORES:
            for start, grad in ((head, dk * SCALE), (HALF_HEADS + head, dv)):
                grad = grad.astype(jnp.bfloat16)
                for device in range(DEVICES):
                    part_ref[PLACE[device], :, start * HEAD_DIM : (start + 1) * HEAD_DIM] = grad[
                        device * SLOTS : (device + 1) * SLOTS
                    ]


def grads_kernel(*refs):
    outs = refs[-2:]
    half = ROWS // 2
    for head, side, (keys, q, do), soft_b, grad_b in Attention(*refs[:6]).units():
        dq_t = dot(keys.T, grad_b, NN) * SCALE
        if side == CORES:
            dq = dq_t.T.astype(jnp.bfloat16)
            for n, out in enumerate(outs):
                for g in range(GROUP):
                    column = (head * GROUP + g) * HEAD_DIM
                    row = (n * GROUP + g) * SLOTS
                    out[PROMPT_ROW:EXTRA_ROW, column : column + HEAD_DIM] = dq[
                        row : row + SLOTS
                    ]
            continue
        out = outs[side]
        for g in range(GROUP):
            column = (head * GROUP + g) * HEAD_DIM
            block = dq_t[:, g * ROWS : (g + 1) * ROWS]
            out[:ROWS, column : column + HEAD_DIM] = block.T.astype(jnp.bfloat16)
        own_dk = (dot(grad_b[KEYS:], q, NN) * SCALE).astype(jnp.bfloat16)
        own_dv = dot(soft_b[KEYS:], do, NN).astype(jnp.bfloat16)
        for n, grad in enumerate((own_dk, own_dv)):
            for part in range(2):
                column = (2 * n + part) * HALF_WIDTH + head * HEAD_DIM
                out[EXTRA_ROW:OTHER_BLOCK, column : column + HEAD_DIM] = grad[
                    part * half : (part + 1) * half
                ]


def join_kernel(mine_ref, got_ref, pdq_ref, cdq_ref, cdk_ref, cdv_ref, sems):
    core = own_core()
    copies = []
    for n, (source, half) in enumerate(((mine_ref, core), (got_ref, 1 - core))):
        wide, narrow = columns_of(half, HALF_COLUMNS), columns_of(half, HALF_WIDTH)
        pairs = [
            (source.at[:ROWS], cdq_ref.at[:, wide]),
            (source.at[PROMPT_ROW:EXTRA_ROW], pdq_ref.at[:, wide]),
        ]
        for k, target in enumerate((cdk_ref, cdv_ref)):
            for part in range(2):
                rows = slice(part * ROWS // 2, (part + 1) * ROWS // 2)
                pairs.append((packed(source, 2 * k + part), target.at[rows, narrow]))
        copies += [
            pltpu.make_async_copy(place, target, sems.at[n * len(pairs) + k])
            for k, (place, target) in enumerate(pairs)
        ]
    run(copies)


def total_kernel(terms_ref, dk_ref, dv_ref):
    for core in range(CORES):
        total = sum(
            terms_ref[PLACE[chip * CORES + core]].astype(jnp.float32) for chip in range(CHIPS)
        ).astype(jnp.bfloat16)
        columns = slice(core * HALF_WIDTH, (core + 1) * HALF_WIDTH)
        dk_ref[:, columns] = total[:, :HALF_WIDTH]
        dv_ref[:, columns] = total[:, HALF_WIDTH:]


def kernel(body, name, shapes, in_specs, out_specs, limit, cost, scratch=()):
    flops, moved, transcendentals = cost
    return pl.pallas_call(
        body,
        out_shape=tuple(jax.ShapeDtypeStruct(shape, jnp.bfloat16) for shape in shapes),
        in_specs=in_specs,
        out_specs=out_specs,
        scratch_shapes=list(scratch),
        compiler_params=pltpu.CompilerParams(vmem_limit_bytes=limit * 1024 * 1024),
        cost_estimate=pl.CostEstimate(
            flops=flops, bytes_accessed=moved, transcendentals=transcendentals
        ),
        name=name,
    )


def in_hbm(*arrays):
    return [pltpu.with_memory_space_constraint(a, pltpu.HBM) for a in arrays]


def body(
    prompt_q,
    prompt_k,
    prompt_value_rows,
    prompt_dout,
    comp_q,
    completion_keys,
    completion_values,
    comp_dout,
    comp_lengths,
    prompt_length,
):
    block = (DEVICES, SLOTS, 2 * HALF_WIDTH)
    queries = (QUERY_BLOCK, HALF_COLUMNS)
    others = (OTHER_BLOCK, HALF_COLUMNS)
    swap = [(device, device ^ 1) for device in range(DEVICES)]

    def exchange(blocks):
        return lax.all_to_all(
            blocks, "sample", split_axis=0, concat_axis=0, axis_index_groups=[ORDER], tiled=True
        )

    (outgoing,) = kernel(
        stage_kernel,
        "stage",
        [block],
        [ANY] * 2,
        (VMEM,),
        4,
        (0, 300_000, 0),
        [
            pltpu.VMEM((2, SLOTS, KEY_VALUE_HEADS * HEAD_DIM), jnp.bfloat16),
            pltpu.SemaphoreType.DMA((2,)),
        ],
    )(*in_hbm(prompt_k, prompt_value_rows))
    kv = exchange(outgoing)
    mine_q, mine_other, their_q, their_other = kernel(
        split_kernel,
        "split",
        [queries, others] * 2,
        [SMEM] + [ANY] * 7,
        (VMEM,) * 4,
        8,
        (0, 3_000_000, 0),
        [pltpu.SemaphoreType.DMA((16,))],
    )(
        comp_lengths,
        *in_hbm(
            comp_q[0],
            comp_dout[0],
            prompt_q,
            prompt_dout,
            completion_keys[0],
            completion_values[0],
        ),
        outgoing,
    )
    got_q = lax.ppermute(their_q, "sample", swap)
    got_other = lax.ppermute(their_other, "sample", swap)
    scores_in = prompt_length, mine_q, mine_other, got_q, got_other, kv
    shares = [
        pl.pallas_call(
            own_kernel,
            out_shape=jax.ShapeDtypeStruct((HALF_HEADS, 8, GROUP * ROWS), jnp.float32),
            in_specs=[VMEM] * 2,
            out_specs=VMEM,
            compiler_params=pltpu.CompilerParams(vmem_limit_bytes=16 * 1024 * 1024),
            cost_estimate=pl.CostEstimate(
                flops=1_000_000, bytes_accessed=300_000, transcendentals=0
            ),
            name="own",
        )(*blocks)
        for blocks in ((mine_q, mine_other), (got_q, got_other))
    ]
    cost = (1_000_000_000, 4_000_000, 850_000)
    (partial,) = kernel(
        attend_kernel, "attend", [block], [SMEM] + [VMEM] * 7, (VMEM,), 24, cost
    )(*scores_in, *shares)
    terms = exchange(partial)
    mine_out, theirs_out = kernel(
        grads_kernel, "grads", [others] * 2, [SMEM] + [VMEM] * 5 + [ANY], (VMEM,) * 2, 24, cost
    )(*scores_in, partial)
    got_out = lax.ppermute(theirs_out, "sample", swap)
    width = KEY_VALUE_HEADS * HEAD_DIM
    shapes = (
        (SLOTS, QUERY_HEADS * HEAD_DIM),
        (ROWS, QUERY_HEADS * HEAD_DIM),
        (ROWS, width),
        (ROWS, width),
    )
    pdq, cdq, cdk, cdv = kernel(
        join_kernel,
        "join",
        shapes,
        [VMEM] * 2,
        (ANY,) * 4,
        4,
        (0, 1_700_000, 0),
        [pltpu.SemaphoreType.DMA((12,))],
    )(mine_out, got_out)
    pdk, pdv = kernel(
        total_kernel, "total", [(SLOTS, width)] * 2, [VMEM], (VMEM,) * 2, 4, (130_000, 300_000, 0)
    )(terms)
    return (pdq, pdk, pdv, cdq[None], cdk[None], cdv[None])


def solution(mesh):
    rows = P(("prompt", "sample"), None)
    blocks = P(("prompt", "sample"), None, None)
    in_specs = (rows,) * 4 + (blocks,) * 4 + (P(("prompt", "sample")), P("prompt"))
    out_specs = (rows,) * 3 + (blocks,) * 3
    return jax.shard_map(body, mesh=mesh, in_specs=in_specs, out_specs=out_specs, check_vma=False)
```

profile of v0, /device:TPU:1, one launch (start us, length us, event | category | flops | bytes accessed | tf_op | source)
XLA Modules:
  0.0 41.2 jit_solution(280981988855780554)
XLA Ops:
  0.6 1.5 %stage.1._ = bf16[16,16,512]{2,1,0:T(8,128)(2,1)} custom-call(bf16[16,512]{1,0:T(8,128)(2,1)} %k_ref.1, bf16[16,512]{1,0:T(8,128)(2,1)} %v_ref.1), custom_call_target="tpu_custom_call" | custom-call | bytes 300000 | tf_op jit(solution)/shard_map/stage/pallas_call | solution.py:381
  2.1 10.3 %all-to-all-start = ((bf16[16,16,512]{2,1,0:T(8,128)(2,1)}), bf16[16,16,512]{2,1,0:T(8,128)(2,1)S(1)}, u32[]{:S(2)}, u32[]{:S(2)}) async-start(bf16[16,16,512]{2,1,0:T(8,128)(2,1)} %stage.1._), calls=%async_computation | async-start | bytes 524288 | tf_op jit(solution)/shard_map/all_to_all | solution.py:377
  13.0 1.5 %split.1 = (bf16[160,1024]{1,0:T(8,128)(2,1)S(1)}, bf16[208,1024]{1,0:T(8,128)(2,1)S(1)}, bf16[160,1024]{1,0:T(8,128)(2,1)S(1)}, bf16[208,1024]{1,0:T(8,128)(2,1)S(1)}) custom-call(s32[1]{0:T(128)S(6)} %copy.16.clen_ref, bf16[128,2048]{1,0:T(8,128)(2,1)} %bitcast.7, bf16[128,2048]{1,0:T(8,128)(2,1)} %bitcast.8, bf16[16,2048]{1,0:T(8,128)(2,1)} %pq_ref.1, ...), custom_call_target="tpu_custom_call" | custom-call | bytes 3000000 | tf_op jit(solution)/shard_map/split/pallas_call | solution.py:395
  14.5 2.1 %collective-permute-start.1 = (bf16[208,1024]{1,0:T(8,128)(2,1)S(1)}, bf16[208,1024]{1,0:T(8,128)(2,1)S(1)}, u32[]{:S(2)}, u32[]{:S(2)}) collective-permute-start(bf16[208,1024]{1,0:T(8,128)(2,1)S(1)} %get-tuple-element.21), channel_id=1, source_target_pairs={{0,1},{1,0},{2,3},{3,2},{4,5},{5,4},{6,7},{7,6},{8,9},{9,8},{10,11... | collective-permute-start | bytes 1277960 | tf_op jit(solution)/shard_map/ppermute | solution.py:417
  16.6 2.3 %collective-permute-start = (bf16[160,1024]{1,0:T(8,128)(2,1)S(1)}, bf16[160,1024]{1,0:T(8,128)(2,1)S(1)}, u32[]{:S(2)}, u32[]{:S(2)}) collective-permute-start(bf16[160,1024]{1,0:T(8,128)(2,1)S(1)} %get-tuple-element.20), channel_id=1, source_target_pairs={{0,1},{1,0},{2,3},{3,2},{4,5},{5,4},{6,7},{7,6},{8,9},{9,8},{10,11... | collective-permute-start | bytes 983048 | tf_op jit(solution)/shard_map/ppermute | solution.py:416
  19.5 0.4 own.2.refs_6_
  19.9 0.2 collective-permute-done.query_block.refs_3_
  20.1 0.0 collective-permute-done.1.other_block.refs_4_
  20.1 0.4 own.3.refs_7_
  20.5 1.8 %all-to-all-done.refs_5_ = bf16[16,16,512]{2,1,0:T(8,128)(2,1)S(1)} async-done(((bf16[16,16,512]{2,1,0:T(8,128)(2,1)}), bf16[16,16,512]{2,1,0:T(8,128)(2,1)S(1)}, u32[]{:S(2)}, u32[]{:S(2)}) %all-to-all-start) | async-done | bytes 262176 | tf_op jit(solution)/shard_map/all_to_all | solution.py:377
  22.3 3.0 %attend.1.refs_6_ = bf16[16,16,512]{2,1,0:T(8,128)(2,1)} custom-call(s32[1]{0:T(128)S(6)} %copy.17.refs_0_, bf16[160,1024]{1,0:T(8,128)(2,1)S(1)} %get-tuple-element.18.query_block.refs_1_, bf16[208,1024]{1,0:T(8,128)(2,1)S(1)} %get-tuple-element.19.other_block.refs_2_, bf16[160,1024]{1,0:T(8,128)(2,1)S(1)} %collective-permute-done.query_block.refs_3_, ...), custom_call_target="tpu_custom_call" | custom-call | flops 1000000000 | bytes 4000000 | tf_op jit(solution)/shard_map/attend/pallas_call | solution.py:434
  25.2 5.4 %all-to-all-start.1 = ((bf16[16,16,512]{2,1,0:T(8,128)(2,1)}), bf16[16,16,512]{2,1,0:T(8,128)(2,1)S(1)}, u32[]{:S(2)}, u32[]{:S(2)}) async-start(bf16[16,16,512]{2,1,0:T(8,128)(2,1)} %attend.1.refs_6_), calls=%async_computation.1 | async-start | bytes 524288 | tf_op jit(solution)/shard_map/all_to_all | solution.py:377
  30.7 3.0 %grads.1 = (bf16[208,1024]{1,0:T(8,128)(2,1)S(1)}, bf16[208,1024]{1,0:T(8,128)(2,1)S(1)}) custom-call(s32[1]{0:T(128)S(6)} %copy.17.refs_0_, bf16[160,1024]{1,0:T(8,128)(2,1)S(1)} %get-tuple-element.18.query_block.refs_1_, bf16[208,1024]{1,0:T(8,128)(2,1)S(1)} %get-tuple-element.19.other_block.refs_2_, ...), custom_call_target="tpu_custom_call" | custom-call | flops 1000000000 | bytes 4000000 | tf_op jit(solution)/shard_map/grads/pallas_call | solution.py:438
  33.6 2.0 %collective-permute-start.2 = (bf16[208,1024]{1,0:T(8,128)(2,1)S(1)}, bf16[208,1024]{1,0:T(8,128)(2,1)S(1)}, u32[]{:S(2)}, u32[]{:S(2)}) collective-permute-start(bf16[208,1024]{1,0:T(8,128)(2,1)S(1)} %get-tuple-element.23), channel_id=1, source_target_pairs={{0,1},{1,0},{2,3},{3,2},{4,5},{5,4},{6,7},{7,6},{8,9},{9,8},{10,11... | collective-permute-start | bytes 1277960 | tf_op jit(solution)/shard_map/ppermute | solution.py:441
  35.7 1.6 %collective-permute-done.2.got_ref = bf16[208,1024]{1,0:T(8,128)(2,1)S(1)} collective-permute-done((bf16[208,1024]{1,0:T(8,128)(2,1)S(1)}, bf16[208,1024]{1,0:T(8,128)(2,1)S(1)}, u32[]{:S(2)}, u32[]{:S(2)}) %collective-permute-start.2) | collective-permute-done | bytes 426016 | tf_op jit(solution)/shard_map/ppermute | solution.py:441
  37.3 1.0 %join.1 = (bf16[16,2048]{1,0:T(8,128)(2,1)}, bf16[128,2048]{1,0:T(8,128)(2,1)}, bf16[128,512]{1,0:T(8,128)(2,1)}, bf16[128,512]{1,0:T(8,128)(2,1)}) custom-call(bf16[208,1024]{1,0:T(8,128)(2,1)S(1)} %get-tuple-element.22.mine_ref, bf16[208,1024]{1,0:T(8,128)(2,1)S(1)} %collective-permute-done.2.got_ref), custom_call_target="tpu_custom_call" | custom-call | bytes 1700000 | tf_op jit(solution)/shard_map/join/pallas_call | solution.py:449
  38.3 2.2 %all-to-all-done.1.terms_ref = bf16[16,16,512]{2,1,0:T(8,128)(2,1)S(1)} async-done(((bf16[16,16,512]{2,1,0:T(8,128)(2,1)}), bf16[16,16,512]{2,1,0:T(8,128)(2,1)S(1)}, u32[]{:S(2)}, u32[]{:S(2)}) %all-to-all-start.1) | async-done | bytes 262176 | tf_op jit(solution)/shard_map/all_to_all | solution.py:377
  40.5 0.6 %total.1 = (bf16[16,512]{1,0:T(8,128)(2,1)}, bf16[16,512]{1,0:T(8,128)(2,1)}) custom-call(bf16[16,16,512]{2,1,0:T(8,128)(2,1)S(1)} %all-to-all-done.1.terms_ref), custom_call_target="tpu_custom_call" | custom-call | flops 130000 | bytes 300000 | tf_op jit(solution)/shard_map/total/pallas_call | solution.py:459
Async XLA Ops:
  2.1 20.2 %all-to-all-start = ((bf16[16,16,512]{2,1,0:T(8,128)(2,1)}), bf16[16,16,512]{2,1,0:T(8,128)(2,1)S(1)}, u32[]{:S(2)}, u32[]{:S(2)}) async-start(bf16[16,16,512]{2,1,0:T(8,128)(2,1)} %stage.1._), calls=%async_computation | async-start | bytes 524288 | tf_op jit(solution)/shard_map/all_to_all | solution.py:377
  14.5 5.6 %collective-permute-start.1 = (bf16[208,1024]{1,0:T(8,128)(2,1)S(1)}, bf16[208,1024]{1,0:T(8,128)(2,1)S(1)}, u32[]{:S(2)}, u32[]{:S(2)}) collective-permute-start(bf16[208,1024]{1,0:T(8,128)(2,1)S(1)} %get-tuple-element.21), channel_id=1, source_target_pairs={{0,1},{1,0},{2,3},{3,2},{4,5},{5,4},{6,7},{7,6},{8,9},{9,8},{10,11... | collective-permute-start | bytes 1277960 | tf_op jit(solution)/shard_map/ppermute | solution.py:417
  16.6 3.5 %collective-permute-start = (bf16[160,1024]{1,0:T(8,128)(2,1)S(1)}, bf16[160,1024]{1,0:T(8,128)(2,1)S(1)}, u32[]{:S(2)}, u32[]{:S(2)}) collective-permute-start(bf16[160,1024]{1,0:T(8,128)(2,1)S(1)} %get-tuple-element.20), channel_id=1, source_target_pairs={{0,1},{1,0},{2,3},{3,2},{4,5},{5,4},{6,7},{7,6},{8,9},{9,8},{10,11... | collective-permute-start | bytes 983048 | tf_op jit(solution)/shard_map/ppermute | solution.py:416
  25.2 15.3 %all-to-all-start.1 = ((bf16[16,16,512]{2,1,0:T(8,128)(2,1)}), bf16[16,16,512]{2,1,0:T(8,128)(2,1)S(1)}, u32[]{:S(2)}, u32[]{:S(2)}) async-start(bf16[16,16,512]{2,1,0:T(8,128)(2,1)} %attend.1.refs_6_), calls=%async_computation.1 | async-start | bytes 524288 | tf_op jit(solution)/shard_map/all_to_all | solution.py:377
  33.6 3.7 %collective-permute-start.2 = (bf16[208,1024]{1,0:T(8,128)(2,1)S(1)}, bf16[208,1024]{1,0:T(8,128)(2,1)S(1)}, u32[]{:S(2)}, u32[]{:S(2)}) collective-permute-start(bf16[208,1024]{1,0:T(8,128)(2,1)S(1)} %get-tuple-element.23), channel_id=1, source_target_pairs={{0,1},{1,0},{2,3},{3,2},{4,5},{5,4},{6,7},{7,6},{8,9},{9,8},{10,11... | collective-permute-start | bytes 1277960 | tf_op jit(solution)/shard_map/ppermute | solution.py:441
where the time goes:
time: 41.8 us; the launch traced here: 41.2 us
  starting transfers between devices  22 us (53%)
  Pallas kernels  11.3 us (27%)
  waiting for transfers between devices  5.85 us (14%)
  between operations  2 us (5%)
    all_to_all x2, starting transfers between devices, exchange(): lax.all_to_all(blocks, 'sample', split_axis=0, concat_axis=0, axis_index_...  15.7 us
    all_to_all x2, waiting for transfers between devices, exchange(): lax.all_to_all(blocks, 'sample', split_axis=0, concat_axis=0, axis_index_...  3.99 us
    pallas_call x1, Pallas kernels, body(): kernel(attend_kernel, 'attend', [block], [SMEM] + [VMEM] * 7, (VMEM,), 24...  2.97 us
    pallas_call x1, Pallas kernels, body(): kernel(grads_kernel, 'grads', [others] * 2, [SMEM] + [VMEM] * 5 + [ANY],...  2.96 us
    ppermute x1, starting transfers between devices, body(): got_q = lax.ppermute(their_q, 'sample', swap)  2.26 us
    ppermute x1, starting transfers between devices, body(): got_other = lax.ppermute(their_other, 'sample', swap)  2.07 us
    ppermute x1, starting transfers between devices, body(): got_out = lax.ppermute(theirs_out, 'sample', swap)  2.01 us
    ppermute x1, waiting for transfers between devices, body(): got_out = lax.ppermute(theirs_out, 'sample', swap)  1.65 us
  transfers between devices with their start and end apart: 5, of which 4 were waited for; matrix products, arithmetic and copies ran while one was open for 0% of the time, Pallas kernels for 15%

commit v1 on v0

--- a/solution.py
+++ b/solution.py
@@ -250,30 +250,32 @@
         return [jnp.concatenate(part, axis=1) for part in zip(*pieces)]
 
     def units(self):
-        todo = [(head, side) for head in range(HALF_HEADS) for side in (0, 1, 2)]
-        following = self.products(*todo[0])
+        todo = [(0, CORES)]
+        todo += [(head, side) for head in range(HALF_HEADS) for side in range(CORES)]
+        todo += [(head, CORES) for head in range(1, HALF_HEADS)]
+        ready = [self.products(*unit) for unit in todo[:2]]
         for n, (head, side) in enumerate(todo):
-            scores, soft_grad, operands = following
-            if n + 1 < len(todo):
-                following = self.products(*todo[n + 1])
-            yield head, side, operands, *self.weights(head, side, scores, soft_grad)
+            scores, soft_grad, operands = ready.pop(0)
+            weights = self.weights(head, side, scores, soft_grad)
+            if n + 2 < len(todo):
+                ready.append(self.products(*todo[n + 2]))
+            yield head, side, operands, *weights
 
 
 def attend_kernel(*refs):
     part_ref = refs[-1]
-    dk = dv = None
-    for head, side, (_, q, do), soft_b, grad_b in Attention(*refs[:8]).units():
-        more_dv = dot(soft_b, do, NN)
-        more_dk = dot(grad_b, q, NN)
-        dv = more_dv if side == 0 else dv + more_dv
-        dk = more_dk if side == 0 else dk + more_dk
-        if side == CORES:
-            for start, grad in ((head, dk * SCALE), (HALF_HEADS + head, dv)):
-                grad = grad.astype(jnp.bfloat16)
-                for device in range(DEVICES):
-                    part_ref[PLACE[device], :, start * HEAD_DIM : (start + 1) * HEAD_DIM] = grad[
-                        device * SLOTS : (device + 1) * SLOTS
-                    ]
+    terms = {}
+    for head, _, (_, q, do), soft_b, grad_b in Attention(*refs[:8]).units():
+        terms.setdefault(head, []).append((dot(grad_b, q, NN), dot(soft_b, do, NN)))
+        if len(terms[head]) <= CORES:
+            continue
+        dk, dv = (sum(parts) for parts in zip(*terms[head]))
+        for start, grad in ((head, dk * SCALE), (HALF_HEADS + head, dv)):
+            grad = grad.astype(jnp.bfloat16)
+            for device in range(DEVICES):
+                part_ref[PLACE[device], :, start * HEAD_DIM : (start + 1) * HEAD_DIM] = grad[
+                    device * SLOTS : (device + 1) * SLOTS
+                ]
 
 
 def grads_kernel(*refs):

time: 41.8 us -> 41.8 us (level)
  no operation moved by 1% of the time
where the time goes in v1:
time: 41.8 us; the launch traced here: 41.2 us
  starting transfers between devices  22 us (53%)
  Pallas kernels  11.3 us (27%)
  waiting for transfers between devices  5.91 us (14%)
  between operations  2 us (5%)
    all_to_all x2, starting transfers between devices, exchange(): lax.all_to_all(blocks, 'sample', split_axis=0, concat_axis=0, axis_index_...  15.7 us
    all_to_all x2, waiting for transfers between devices, exchange(): lax.all_to_all(blocks, 'sample', split_axis=0, concat_axis=0, axis_index_...  4.04 us
    pallas_call x1, Pallas kernels, body(): kernel(attend_kernel, 'attend', [block], [SMEM] + [VMEM] * 7, (VMEM,), 24...  3.04 us
    pallas_call x1, Pallas kernels, body(): kernel(grads_kernel, 'grads', [others] * 2, [SMEM] + [VMEM] * 5 + [ANY],...  2.9 us
    ppermute x1, starting transfers between devices, body(): got_q = lax.ppermute(their_q, 'sample', swap)  2.26 us
    ppermute x1, starting transfers between devices, body(): got_other = lax.ppermute(their_other, 'sample', swap)  2.07 us
    ppermute x1, starting transfers between devices, body(): got_out = lax.ppermute(theirs_out, 'sample', swap)  2.01 us
    ppermute x1, waiting for transfers between devices, body(): got_out = lax.ppermute(theirs_out, 'sample', swap)  1.65 us
  transfers between devices with their start and end apart: 5, of which 4 were waited for; matrix products, arithmetic and copies ran while one was open for 0% of the time, Pallas kernels for 15%

profile of v1, /device:TPU:1, one launch (start us, length us, event | category | flops | bytes accessed | tf_op | source)
XLA Modules:
  0.0 41.2 jit_solution(14611222567737609402)
XLA Ops:
  0.6 1.5 %stage.1._ = bf16[16,16,512]{2,1,0:T(8,128)(2,1)} custom-call(bf16[16,512]{1,0:T(8,128)(2,1)} %k_ref.1, bf16[16,512]{1,0:T(8,128)(2,1)} %v_ref.1), custom_call_target="tpu_custom_call" | custom-call | bytes 300000 | tf_op jit(solution)/shard_map/stage/pallas_call | solution.py:383
  2.1 10.3 %all-to-all-start = ((bf16[16,16,512]{2,1,0:T(8,128)(2,1)}), bf16[16,16,512]{2,1,0:T(8,128)(2,1)S(1)}, u32[]{:S(2)}, u32[]{:S(2)}) async-start(bf16[16,16,512]{2,1,0:T(8,128)(2,1)} %stage.1._), calls=%async_computation | async-start | bytes 524288 | tf_op jit(solution)/shard_map/all_to_all | solution.py:379
  13.0 1.5 %split.1 = (bf16[160,1024]{1,0:T(8,128)(2,1)S(1)}, bf16[208,1024]{1,0:T(8,128)(2,1)S(1)}, bf16[160,1024]{1,0:T(8,128)(2,1)S(1)}, bf16[208,1024]{1,0:T(8,128)(2,1)S(1)}) custom-call(s32[1]{0:T(128)S(6)} %copy.16.clen_ref, bf16[128,2048]{1,0:T(8,128)(2,1)} %bitcast.7, bf16[128,2048]{1,0:T(8,128)(2,1)} %bitcast.8, bf16[16,2048]{1,0:T(8,128)(2,1)} %pq_ref.1, ...), custom_call_target="tpu_custom_call" | custom-call | bytes 3000000 | tf_op jit(solution)/shard_map/split/pallas_call | solution.py:397
  14.5 2.1 %collective-permute-start.1 = (bf16[208,1024]{1,0:T(8,128)(2,1)S(1)}, bf16[208,1024]{1,0:T(8,128)(2,1)S(1)}, u32[]{:S(2)}, u32[]{:S(2)}) collective-permute-start(bf16[208,1024]{1,0:T(8,128)(2,1)S(1)} %get-tuple-element.21), channel_id=1, source_target_pairs={{0,1},{1,0},{2,3},{3,2},{4,5},{5,4},{6,7},{7,6},{8,9},{9,8},{10,11... | collective-permute-start | bytes 1277960 | tf_op jit(solution)/shard_map/ppermute | solution.py:419
  16.6 2.3 %collective-permute-start = (bf16[160,1024]{1,0:T(8,128)(2,1)S(1)}, bf16[160,1024]{1,0:T(8,128)(2,1)S(1)}, u32[]{:S(2)}, u32[]{:S(2)}) collective-permute-start(bf16[160,1024]{1,0:T(8,128)(2,1)S(1)} %get-tuple-element.20), channel_id=1, source_target_pairs={{0,1},{1,0},{2,3},{3,2},{4,5},{5,4},{6,7},{7,6},{8,9},{9,8},{10,11... | collective-permute-start | bytes 983048 | tf_op jit(solution)/shard_map/ppermute | solution.py:418
  19.5 0.4 own.2.refs_6_
  19.9 0.2 collective-permute-done.query_block.refs_3_
  20.1 0.0 collective-permute-done.1.other_block.refs_4_
  20.1 0.4 own.3.refs_7_
  20.5 1.8 %all-to-all-done.refs_5_ = bf16[16,16,512]{2,1,0:T(8,128)(2,1)S(1)} async-done(((bf16[16,16,512]{2,1,0:T(8,128)(2,1)}), bf16[16,16,512]{2,1,0:T(8,128)(2,1)S(1)}, u32[]{:S(2)}, u32[]{:S(2)}) %all-to-all-start) | async-done | bytes 262176 | tf_op jit(solution)/shard_map/all_to_all | solution.py:379
  22.3 3.0 %attend.1.refs_6_ = bf16[16,16,512]{2,1,0:T(8,128)(2,1)} custom-call(s32[1]{0:T(128)S(6)} %copy.17.refs_0_, bf16[160,1024]{1,0:T(8,128)(2,1)S(1)} %get-tuple-element.18.query_block.refs_1_, bf16[208,1024]{1,0:T(8,128)(2,1)S(1)} %get-tuple-element.19.other_block.refs_2_, bf16[160,1024]{1,0:T(8,128)(2,1)S(1)} %collective-permute-done.query_block.refs_3_, ...), custom_call_target="tpu_custom_call" | custom-call | flops 1000000000 | bytes 4000000 | tf_op jit(solution)/shard_map/attend/pallas_call | solution.py:436
  25.3 5.4 %all-to-all-start.1 = ((bf16[16,16,512]{2,1,0:T(8,128)(2,1)}), bf16[16,16,512]{2,1,0:T(8,128)(2,1)S(1)}, u32[]{:S(2)}, u32[]{:S(2)}) async-start(bf16[16,16,512]{2,1,0:T(8,128)(2,1)} %attend.1.refs_6_), calls=%async_computation.1 | async-start | bytes 524288 | tf_op jit(solution)/shard_map/all_to_all | solution.py:379
  30.8 2.9 %grads.1 = (bf16[208,1024]{1,0:T(8,128)(2,1)S(1)}, bf16[208,1024]{1,0:T(8,128)(2,1)S(1)}) custom-call(s32[1]{0:T(128)S(6)} %copy.17.refs_0_, bf16[160,1024]{1,0:T(8,128)(2,1)S(1)} %get-tuple-element.18.query_block.refs_1_, bf16[208,1024]{1,0:T(8,128)(2,1)S(1)} %get-tuple-element.19.other_block.refs_2_, ...), custom_call_target="tpu_custom_call" | custom-call | flops 1000000000 | bytes 4000000 | tf_op jit(solution)/shard_map/grads/pallas_call | solution.py:440
  33.7 2.0 %collective-permute-start.2 = (bf16[208,1024]{1,0:T(8,128)(2,1)S(1)}, bf16[208,1024]{1,0:T(8,128)(2,1)S(1)}, u32[]{:S(2)}, u32[]{:S(2)}) collective-permute-start(bf16[208,1024]{1,0:T(8,128)(2,1)S(1)} %get-tuple-element.23), channel_id=1, source_target_pairs={{0,1},{1,0},{2,3},{3,2},{4,5},{5,4},{6,7},{7,6},{8,9},{9,8},{10,11... | collective-permute-start | bytes 1277960 | tf_op jit(solution)/shard_map/ppermute | solution.py:443
  35.7 1.6 %collective-permute-done.2.got_ref = bf16[208,1024]{1,0:T(8,128)(2,1)S(1)} collective-permute-done((bf16[208,1024]{1,0:T(8,128)(2,1)S(1)}, bf16[208,1024]{1,0:T(8,128)(2,1)S(1)}, u32[]{:S(2)}, u32[]{:S(2)}) %collective-permute-start.2) | collective-permute-done | bytes 426016 | tf_op jit(solution)/shard_map/ppermute | solution.py:443
  37.3 1.0 %join.1 = (bf16[16,2048]{1,0:T(8,128)(2,1)}, bf16[128,2048]{1,0:T(8,128)(2,1)}, bf16[128,512]{1,0:T(8,128)(2,1)}, bf16[128,512]{1,0:T(8,128)(2,1)}) custom-call(bf16[208,1024]{1,0:T(8,128)(2,1)S(1)} %get-tuple-element.22.mine_ref, bf16[208,1024]{1,0:T(8,128)(2,1)S(1)} %collective-permute-done.2.got_ref), custom_call_target="tpu_custom_call" | custom-call | bytes 1700000 | tf_op jit(solution)/shard_map/join/pallas_call | solution.py:451
  38.3 2.3 %all-to-all-done.1.terms_ref = bf16[16,16,512]{2,1,0:T(8,128)(2,1)S(1)} async-done(((bf16[16,16,512]{2,1,0:T(8,128)(2,1)}), bf16[16,16,512]{2,1,0:T(8,128)(2,1)S(1)}, u32[]{:S(2)}, u32[]{:S(2)}) %all-to-all-start.1) | async-done | bytes 262176 | tf_op jit(solution)/shard_map/all_to_all | solution.py:379
  40.6 0.6 %total.1 = (bf16[16,512]{1,0:T(8,128)(2,1)}, bf16[16,512]{1,0:T(8,128)(2,1)}) custom-call(bf16[16,16,512]{2,1,0:T(8,128)(2,1)S(1)} %all-to-all-done.1.terms_ref), custom_call_target="tpu_custom_call" | custom-call | flops 130000 | bytes 300000 | tf_op jit(solution)/shard_map/total/pallas_call | solution.py:461
Async XLA Ops:
  2.1 20.2 %all-to-all-start = ((bf16[16,16,512]{2,1,0:T(8,128)(2,1)}), bf16[16,16,512]{2,1,0:T(8,128)(2,1)S(1)}, u32[]{:S(2)}, u32[]{:S(2)}) async-start(bf16[16,16,512]{2,1,0:T(8,128)(2,1)} %stage.1._), calls=%async_computation | async-start | bytes 524288 | tf_op jit(solution)/shard_map/all_to_all | solution.py:379
  14.5 5.6 %collective-permute-start.1 = (bf16[208,1024]{1,0:T(8,128)(2,1)S(1)}, bf16[208,1024]{1,0:T(8,128)(2,1)S(1)}, u32[]{:S(2)}, u32[]{:S(2)}) collective-permute-start(bf16[208,1024]{1,0:T(8,128)(2,1)S(1)} %get-tuple-element.21), channel_id=1, source_target_pairs={{0,1},{1,0},{2,3},{3,2},{4,5},{5,4},{6,7},{7,6},{8,9},{9,8},{10,11... | collective-permute-start | bytes 1277960 | tf_op jit(solution)/shard_map/ppermute | solution.py:419
  16.6 3.5 %collective-permute-start = (bf16[160,1024]{1,0:T(8,128)(2,1)S(1)}, bf16[160,1024]{1,0:T(8,128)(2,1)S(1)}, u32[]{:S(2)}, u32[]{:S(2)}) collective-permute-start(bf16[160,1024]{1,0:T(8,128)(2,1)S(1)} %get-tuple-element.20), channel_id=1, source_target_pairs={{0,1},{1,0},{2,3},{3,2},{4,5},{5,4},{6,7},{7,6},{8,9},{9,8},{10,11... | collective-permute-start | bytes 983048 | tf_op jit(solution)/shard_map/ppermute | solution.py:418
  25.3 15.3 %all-to-all-start.1 = ((bf16[16,16,512]{2,1,0:T(8,128)(2,1)}), bf16[16,16,512]{2,1,0:T(8,128)(2,1)S(1)}, u32[]{:S(2)}, u32[]{:S(2)}) async-start(bf16[16,16,512]{2,1,0:T(8,128)(2,1)} %attend.1.refs_6_), calls=%async_computation.1 | async-start | bytes 524288 | tf_op jit(solution)/shard_map/all_to_all | solution.py:379
  33.7 3.7 %collective-permute-start.2 = (bf16[208,1024]{1,0:T(8,128)(2,1)S(1)}, bf16[208,1024]{1,0:T(8,128)(2,1)S(1)}, u32[]{:S(2)}, u32[]{:S(2)}) collective-permute-start(bf16[208,1024]{1,0:T(8,128)(2,1)S(1)} %get-tuple-element.23), channel_id=1, source_target_pairs={{0,1},{1,0},{2,3},{3,2},{4,5},{5,4},{6,7},{7,6},{8,9},{9,8},{10,11... | collective-permute-start | bytes 1277960 | tf_op jit(solution)/shard_map/ppermute | solution.py:443

commit v2 on v0

--- a/solution.py
+++ b/solution.py
@@ -63,18 +63,28 @@
         copy.wait()
 
 
-def stage_kernel(k_ref, v_ref, out_ref, kv_ref, sems):
+def stage_kernel(k_ref, v_ref, out_ref, kv_ref, blocks_ref, sems):
     run(
         [
             pltpu.make_async_copy(source, kv_ref.at[n], sems.at[n])
             for n, source in enumerate((k_ref, v_ref))
         ]
     )
+    halves = []
     for core in range(CORES):
         columns = slice(core * HALF_WIDTH, (core + 1) * HALF_WIDTH)
-        rows = jnp.concatenate([kv_ref[0, :, columns], kv_ref[1, :, columns]], axis=1)
-        for chip in range(CHIPS):
-            out_ref[PLACE[chip * CORES + core]] = rows
+        halves.append(jnp.concatenate([kv_ref[0, :, columns], kv_ref[1, :, columns]], axis=1))
+    copies = []
+    for first in range(0, DEVICES, 4):
+        for place in range(first, first + 4):
+            blocks_ref[place] = halves[ORDER[place] % CORES]
+        copy = pltpu.make_async_copy(
+            blocks_ref.at[first : first + 4], out_ref.at[first : first + 4], sems.at[2 + first // 4]
+        )
+        copy.start()
+        copies.append(copy)
+    for copy in copies:
+        copy.wait()
 
 
 def packed(ref, n):
@@ -260,8 +270,9 @@
 
 
 def attend_kernel(*refs):
-    part_ref = refs[-1]
+    part_ref, blocks_ref, sems = refs[8:]
     dk = dv = None
+    copies = []
     for head, side, (_, q, do), soft_b, grad_b in Attention(*refs[:8]).units():
         more_dv = dot(soft_b, do, NN)
         more_dk = dot(grad_b, q, NN)
@@ -271,9 +282,16 @@
             for start, grad in ((head, dk * SCALE), (HALF_HEADS + head, dv)):
                 grad = grad.astype(jnp.bfloat16)
                 for device in range(DEVICES):
-                    part_ref[PLACE[device], :, start * HEAD_DIM : (start + 1) * HEAD_DIM] = grad[
-                        device * SLOTS : (device + 1) * SLOTS
-                    ]
+                    blocks_ref[start, PLACE[device]] = grad[device * SLOTS : (device + 1) * SLOTS]
+                copy = pltpu.make_async_copy(
+                    blocks_ref.at[start],
+                    part_ref.at[:, :, start * HEAD_DIM : (start + 1) * HEAD_DIM],
+                    sems.at[start],
+                )
+                copy.start()
+                copies.append(copy)
+    for copy in copies:
+        copy.wait()
 
 
 def grads_kernel(*refs):
@@ -383,12 +401,13 @@
         "stage",
         [block],
         [ANY] * 2,
-        (VMEM,),
+        (ANY,),
         4,
         (0, 300_000, 0),
         [
             pltpu.VMEM((2, SLOTS, KEY_VALUE_HEADS * HEAD_DIM), jnp.bfloat16),
-            pltpu.SemaphoreType.DMA((2,)),
+            pltpu.VMEM(block, jnp.bfloat16),
+            pltpu.SemaphoreType.DMA((2 + DEVICES // 4,)),
         ],
     )(*in_hbm(prompt_k, prompt_value_rows))
     kv = exchange(outgoing)
@@ -432,7 +451,17 @@
     ]
     cost = (1_000_000_000, 4_000_000, 850_000)
     (partial,) = kernel(
-        attend_kernel, "attend", [block], [SMEM] + [VMEM] * 7, (VMEM,), 24, cost
+        attend_kernel,
+        "attend",
+        [block],
+        [SMEM] + [VMEM] * 7,
+        (ANY,),
+        24,
+        cost,
+        [
+            pltpu.VMEM((2 * HALF_HEADS, DEVICES, SLOTS, HEAD_DIM), jnp.bfloat16),
+            pltpu.SemaphoreType.DMA((2 * HALF_HEADS,)),
+        ],
     )(*scores_in, *shares)
     terms = exchange(partial)
     mine_out, theirs_out = kernel(

time: 41.8 us -> 41.8 us (level)
  no operation moved by 1% of the time
where the time goes in v2:
time: 41.8 us; the launch traced here: 41.2 us
  starting transfers between devices  22.1 us (53%)
  Pallas kernels  11.3 us (27%)
  waiting for transfers between devices  5.85 us (14%)
  between operations  2.01 us (5%)
    all_to_all x2, starting transfers between devices, exchange(): lax.all_to_all(blocks, 'sample', split_axis=0, concat_axis=0, axis_index_...  15.7 us
    all_to_all x2, waiting for transfers between devices, exchange(): lax.all_to_all(blocks, 'sample', split_axis=0, concat_axis=0, axis_index_...  3.98 us
    pallas_call x1, Pallas kernels, body(): kernel(grads_kernel, 'grads', [others] * 2, [SMEM] + [VMEM] * 5 + [ANY],...  2.97 us
    pallas_call x1, Pallas kernels, body(): kernel(attend_kernel, 'attend', [block], [SMEM] + [VMEM] * 7, (ANY,), 24,...  2.96 us
    ppermute x1, starting transfers between devices, body(): got_q = lax.ppermute(their_q, 'sample', swap)  2.26 us
    ppermute x1, starting transfers between devices, body(): got_other = lax.ppermute(their_other, 'sample', swap)  2.07 us
    ppermute x1, starting transfers between devices, body(): got_out = lax.ppermute(theirs_out, 'sample', swap)  2.01 us
    ppermute x1, waiting for transfers between devices, body(): got_out = lax.ppermute(theirs_out, 'sample', swap)  1.65 us
  transfers between devices with their start and end apart: 5, of which 4 were waited for; matrix products, arithmetic and copies ran while one was open for 0% of the time, Pallas kernels for 15%

profile of v2, /device:TPU:1, one launch (start us, length us, event | category | flops | bytes accessed | tf_op | source)
XLA Modules:
  0.0 41.2 jit_solution(13078241098899179461)
XLA Ops:
  0.6 1.5 %stage.1._ = bf16[16,16,512]{2,1,0:T(8,128)(2,1)} custom-call(bf16[16,512]{1,0:T(8,128)(2,1)} %k_ref.1, bf16[16,512]{1,0:T(8,128)(2,1)} %v_ref.1), custom_call_target="tpu_custom_call" | custom-call | bytes 300000 | tf_op jit(solution)/shard_map/stage/pallas_call | solution.py:399
  2.1 10.3 %all-to-all-start = ((bf16[16,16,512]{2,1,0:T(8,128)(2,1)}), bf16[16,16,512]{2,1,0:T(8,128)(2,1)S(1)}, u32[]{:S(2)}, u32[]{:S(2)}) async-start(bf16[16,16,512]{2,1,0:T(8,128)(2,1)} %stage.1._), calls=%async_computation | async-start | bytes 524288 | tf_op jit(solution)/shard_map/all_to_all | solution.py:395
  13.0 1.5 %split.1 = (bf16[160,1024]{1,0:T(8,128)(2,1)S(1)}, bf16[208,1024]{1,0:T(8,128)(2,1)S(1)}, bf16[160,1024]{1,0:T(8,128)(2,1)S(1)}, bf16[208,1024]{1,0:T(8,128)(2,1)S(1)}) custom-call(s32[1]{0:T(128)S(6)} %copy.16.clen_ref, bf16[128,2048]{1,0:T(8,128)(2,1)} %bitcast.7, bf16[128,2048]{1,0:T(8,128)(2,1)} %bitcast.8, bf16[16,2048]{1,0:T(8,128)(2,1)} %pq_ref.1, ...), custom_call_target="tpu_custom_call" | custom-call | bytes 3000000 | tf_op jit(solution)/shard_map/split/pallas_call | solution.py:414
  14.5 2.1 %collective-permute-start.1 = (bf16[208,1024]{1,0:T(8,128)(2,1)S(1)}, bf16[208,1024]{1,0:T(8,128)(2,1)S(1)}, u32[]{:S(2)}, u32[]{:S(2)}) collective-permute-start(bf16[208,1024]{1,0:T(8,128)(2,1)S(1)} %get-tuple-element.21), channel_id=1, source_target_pairs={{0,1},{1,0},{2,3},{3,2},{4,5},{5,4},{6,7},{7,6},{8,9},{9,8},{10,11... | collective-permute-start | bytes 1277960 | tf_op jit(solution)/shard_map/ppermute | solution.py:436
  16.6 2.3 %collective-permute-start = (bf16[160,1024]{1,0:T(8,128)(2,1)S(1)}, bf16[160,1024]{1,0:T(8,128)(2,1)S(1)}, u32[]{:S(2)}, u32[]{:S(2)}) collective-permute-start(bf16[160,1024]{1,0:T(8,128)(2,1)S(1)} %get-tuple-element.20), channel_id=1, source_target_pairs={{0,1},{1,0},{2,3},{3,2},{4,5},{5,4},{6,7},{7,6},{8,9},{9,8},{10,11... | collective-permute-start | bytes 983048 | tf_op jit(solution)/shard_map/ppermute | solution.py:435
  19.5 0.4 own.2.refs_6_
  19.9 0.2 collective-permute-done.query_block.refs_3_
  20.1 0.0 collective-permute-done.1.other_block.refs_4_
  20.1 0.4 own.3.refs_7_
  20.5 1.8 %all-to-all-done.refs_5_ = bf16[16,16,512]{2,1,0:T(8,128)(2,1)S(1)} async-done(((bf16[16,16,512]{2,1,0:T(8,128)(2,1)}), bf16[16,16,512]{2,1,0:T(8,128)(2,1)S(1)}, u32[]{:S(2)}, u32[]{:S(2)}) %all-to-all-start) | async-done | bytes 262176 | tf_op jit(solution)/shard_map/all_to_all | solution.py:395
  22.3 3.0 %attend.1.refs_6_ = bf16[16,16,512]{2,1,0:T(8,128)(2,1)} custom-call(s32[1]{0:T(128)S(6)} %copy.17.refs_0_, bf16[160,1024]{1,0:T(8,128)(2,1)S(1)} %get-tuple-element.18.query_block.refs_1_, bf16[208,1024]{1,0:T(8,128)(2,1)S(1)} %get-tuple-element.19.other_block.refs_2_, bf16[160,1024]{1,0:T(8,128)(2,1)S(1)} %collective-permute-done.query_block.refs_3_, ...), custom_call_target="tpu_custom_call" | custom-call | flops 1000000000 | bytes 4000000 | tf_op jit(solution)/shard_map/attend/pallas_call | solution.py:453
  25.3 5.5 %all-to-all-start.1 = ((bf16[16,16,512]{2,1,0:T(8,128)(2,1)}), bf16[16,16,512]{2,1,0:T(8,128)(2,1)S(1)}, u32[]{:S(2)}, u32[]{:S(2)}) async-start(bf16[16,16,512]{2,1,0:T(8,128)(2,1)} %attend.1.refs_6_), calls=%async_computation.1 | async-start | bytes 524288 | tf_op jit(solution)/shard_map/all_to_all | solution.py:395
  30.7 3.0 %grads.1 = (bf16[208,1024]{1,0:T(8,128)(2,1)S(1)}, bf16[208,1024]{1,0:T(8,128)(2,1)S(1)}) custom-call(s32[1]{0:T(128)S(6)} %copy.17.refs_0_, bf16[160,1024]{1,0:T(8,128)(2,1)S(1)} %get-tuple-element.18.query_block.refs_1_, bf16[208,1024]{1,0:T(8,128)(2,1)S(1)} %get-tuple-element.19.other_block.refs_2_, ...), custom_call_target="tpu_custom_call" | custom-call | flops 1000000000 | bytes 4000000 | tf_op jit(solution)/shard_map/grads/pallas_call | solution.py:467
  33.7 2.0 %collective-permute-start.2 = (bf16[208,1024]{1,0:T(8,128)(2,1)S(1)}, bf16[208,1024]{1,0:T(8,128)(2,1)S(1)}, u32[]{:S(2)}, u32[]{:S(2)}) collective-permute-start(bf16[208,1024]{1,0:T(8,128)(2,1)S(1)} %get-tuple-element.23), channel_id=1, source_target_pairs={{0,1},{1,0},{2,3},{3,2},{4,5},{5,4},{6,7},{7,6},{8,9},{9,8},{10,11... | collective-permute-start | bytes 1277960 | tf_op jit(solution)/shard_map/ppermute | solution.py:470
  35.7 1.6 %collective-permute-done.2.got_ref = bf16[208,1024]{1,0:T(8,128)(2,1)S(1)} collective-permute-done((bf16[208,1024]{1,0:T(8,128)(2,1)S(1)}, bf16[208,1024]{1,0:T(8,128)(2,1)S(1)}, u32[]{:S(2)}, u32[]{:S(2)}) %collective-permute-start.2) | collective-permute-done | bytes 426016 | tf_op jit(solution)/shard_map/ppermute | solution.py:470
  37.4 1.0 %join.1 = (bf16[16,2048]{1,0:T(8,128)(2,1)}, bf16[128,2048]{1,0:T(8,128)(2,1)}, bf16[128,512]{1,0:T(8,128)(2,1)}, bf16[128,512]{1,0:T(8,128)(2,1)}) custom-call(bf16[208,1024]{1,0:T(8,128)(2,1)S(1)} %get-tuple-element.22.mine_ref, bf16[208,1024]{1,0:T(8,128)(2,1)S(1)} %collective-permute-done.2.got_ref), custom_call_target="tpu_custom_call" | custom-call | bytes 1700000 | tf_op jit(solution)/shard_map/join/pallas_call | solution.py:478
  38.3 2.2 %all-to-all-done.1.terms_ref = bf16[16,16,512]{2,1,0:T(8,128)(2,1)S(1)} async-done(((bf16[16,16,512]{2,1,0:T(8,128)(2,1)}), bf16[16,16,512]{2,1,0:T(8,128)(2,1)S(1)}, u32[]{:S(2)}, u32[]{:S(2)}) %all-to-all-start.1) | async-done | bytes 262176 | tf_op jit(solution)/shard_map/all_to_all | solution.py:395
  40.5 0.6 %total.1 = (bf16[16,512]{1,0:T(8,128)(2,1)}, bf16[16,512]{1,0:T(8,128)(2,1)}) custom-call(bf16[16,16,512]{2,1,0:T(8,128)(2,1)S(1)} %all-to-all-done.1.terms_ref), custom_call_target="tpu_custom_call" | custom-call | flops 130000 | bytes 300000 | tf_op jit(solution)/shard_map/total/pallas_call | solution.py:488
Async XLA Ops:
  2.1 20.2 %all-to-all-start = ((bf16[16,16,512]{2,1,0:T(8,128)(2,1)}), bf16[16,16,512]{2,1,0:T(8,128)(2,1)S(1)}, u32[]{:S(2)}, u32[]{:S(2)}) async-start(bf16[16,16,512]{2,1,0:T(8,128)(2,1)} %stage.1._), calls=%async_computation | async-start | bytes 524288 | tf_op jit(solution)/shard_map/all_to_all | solution.py:395
  14.5 5.6 %collective-permute-start.1 = (bf16[208,1024]{1,0:T(8,128)(2,1)S(1)}, bf16[208,1024]{1,0:T(8,128)(2,1)S(1)}, u32[]{:S(2)}, u32[]{:S(2)}) collective-permute-start(bf16[208,1024]{1,0:T(8,128)(2,1)S(1)} %get-tuple-element.21), channel_id=1, source_target_pairs={{0,1},{1,0},{2,3},{3,2},{4,5},{5,4},{6,7},{7,6},{8,9},{9,8},{10,11... | collective-permute-start | bytes 1277960 | tf_op jit(solution)/shard_map/ppermute | solution.py:436
  16.6 3.5 %collective-permute-start = (bf16[160,1024]{1,0:T(8,128)(2,1)S(1)}, bf16[160,1024]{1,0:T(8,128)(2,1)S(1)}, u32[]{:S(2)}, u32[]{:S(2)}) collective-permute-start(bf16[160,1024]{1,0:T(8,128)(2,1)S(1)} %get-tuple-element.20), channel_id=1, source_target_pairs={{0,1},{1,0},{2,3},{3,2},{4,5},{5,4},{6,7},{7,6},{8,9},{9,8},{10,11... | collective-permute-start | bytes 983048 | tf_op jit(solution)/shard_map/ppermute | solution.py:435
  25.3 15.3 %all-to-all-start.1 = ((bf16[16,16,512]{2,1,0:T(8,128)(2,1)}), bf16[16,16,512]{2,1,0:T(8,128)(2,1)S(1)}, u32[]{:S(2)}, u32[]{:S(2)}) async-start(bf16[16,16,512]{2,1,0:T(8,128)(2,1)} %attend.1.refs_6_), calls=%async_computation.1 | async-start | bytes 524288 | tf_op jit(solution)/shard_map/all_to_all | solution.py:395
  33.7 3.7 %collective-permute-start.2 = (bf16[208,1024]{1,0:T(8,128)(2,1)S(1)}, bf16[208,1024]{1,0:T(8,128)(2,1)S(1)}, u32[]{:S(2)}, u32[]{:S(2)}) collective-permute-start(bf16[208,1024]{1,0:T(8,128)(2,1)S(1)} %get-tuple-element.23), channel_id=1, source_target_pairs={{0,1},{1,0},{2,3},{3,2},{4,5},{5,4},{6,7},{7,6},{8,9},{9,8},{10,11... | collective-permute-start | bytes 1277960 | tf_op jit(solution)/shard_map/ppermute | solution.py:470
